TPU v7x, 128 devices: a whole 4x4x4 slice. The times are simulated.
128 devices in a mesh: island: 4 (over x_hi, core), fsdp: 32 (over y, x_lo, z).
Axes of the slice: x: 4 (x_hi: 2, x_lo: 2; x = x_hi * 2 + x_lo), y: 4, z: 4, core: 2. Of those that a mesh axis runs over, the one named last changes fastest.
Arguments:
- hidden_acts: bfloat16 [114688, 7168], P(('island', 'fsdp')), may hold values from -24 to 24
- output_grads: bfloat16 [114688, 2048], P(('island', 'fsdp')), may hold values from -0.03540039 to 0.03540039
- island_drift: float32 [4, 7168, 2048], P('island', 'fsdp'), may hold values from -6 to 6
- master_weights: float32 [7168, 2048], P('fsdp'), may hold values from -3 to 3
- momentum: float32 [7168, 2048], P('fsdp'), may hold values from -3 to 3
- mixture: int32 [4], replicated, may hold values from 1 to 128
- denominator: int32 [1], replicated, may hold values from 256 to 1024
Outputs:
- new_weights: bfloat16 [7168, 2048], P('fsdp')
- new_momentum: float32 [7168, 2048], P('fsdp')
All inputs are finite; a program needn't handle non-finite values.
Results may differ from a plain program's by a relative error of at most 0.017.
Values may be sent and summed in bfloat16 or wider, within the bound.
No kernel may reach another device: no remote copies, remote signals or barrier semaphores. Data moves between devices by JAX's collectives and lax.ppermute only.
A program may use at most 128 MiB of HBM per device.

v0:
```python
import jax
import jax.numpy as jnp
from jax import lax
from jax.sharding import PartitionSpec as P

inner_rate = 0.5
outer_decay = 0.9
outer_rate = 0.7


def body(hidden_acts, output_grads, island_drift, master_weights, momentum, mixture, denominator):
    product = lax.dot_general(
        hidden_acts, output_grads, (((0,), (0,)), ((), ())), preferred_element_type=jnp.float32
    )
    gradient = lax.psum_scatter(
        product.astype(jnp.bfloat16), "fsdp", scatter_dimension=0, tiled=True
    ).astype(jnp.float32)
    pseudo = island_drift[0] + inner_rate * gradient
    island = lax.axis_index("island")
    island_count = lax.axis_size("island")
    picked = jnp.where(jnp.arange(island_count, dtype=jnp.int32) == island, mixture, 0)
    weighted = jnp.sum(picked).astype(jnp.float32) * pseudo
    divisor = denominator[0].astype(jnp.float32)
    combined = (
        lax.psum_scatter(
            weighted.astype(jnp.bfloat16), "island", scatter_dimension=1, tiled=True
        ).astype(jnp.float32)
        / divisor
    )
    col_width = combined.shape[1]
    col_start = island * col_width
    master_part = lax.dynamic_slice_in_dim(master_weights, col_start, col_width, 1)
    moment_part = lax.dynamic_slice_in_dim(momentum, col_start, col_width, 1)
    new_moment = outer_decay * moment_part + combined
    new_master = master_part - outer_rate * (combined + outer_decay * new_moment)
    full_master, full_moment = (
        lax.all_gather(new_master.astype(jnp.bfloat16), "island", axis=1, tiled=True).astype(
            new_master.dtype
        ),
        lax.all_gather(new_moment.astype(jnp.bfloat16), "island", axis=1, tiled=True).astype(
            new_moment.dtype
        ),
    )
    return (full_master.astype(jnp.bfloat16), full_moment)


def solution(mesh):
    in_specs = (
        P(("island", "fsdp"), None),
        P(("island", "fsdp"), None),
        P("island", "fsdp", None),
        P("fsdp", None),
        P("fsdp", None),
        P(),
        P(),
    )
    out_specs = (P("fsdp", None), P("fsdp", None))
    return jax.shard_map(body, mesh=mesh, in_specs=in_specs, out_specs=out_specs, check_vma=False)
```

profile of v0, /device:TPU:1, one launch (start us, length us, event | category | flops | bytes accessed | tf_op | source)
XLA Modules:
  0.0 434.4 jit_solution(1984766160207675726)
XLA Ops:
  7.2 0.0 reduce-scatter.3.cloned.1.call-start
  7.2 39.4 %convolution_convert_fusion = bf16[7168,2048]{1,0:T(8,128)(2,1)} fusion(bf16[896,7168]{1,0:T(8,128)(2,1)} %param.7, bf16[896,2048]{1,0:T(8,128)(2,1)} %param.8), kind=kOutput, calls=%fused_computation | convolution fusion | flops 26321354752 | bytes 45875200 | tf_op jit(solution)/shard_map/dot_general | solution.py:12
  46.7 0.0 copy-start.1
  46.7 0.0 copy-start
  46.7 0.0 reduce-scatter.3.cloned.1.call-update
  46.7 0.0 reduce-scatter.5.cloned.1.call-start
  46.7 0.6 copy-done.1
  47.3 0.6 fusion.3
  48.6 322.6 %reduce-scatter.3.cloned.1.call-done = bf16[224,2048]{1,0:T(8,128)(2,1)} async-done(((bf16[7168,2048]{1,0:T(8,128)(2,1)}), bf16[224,2048]{1,0:T(8,128)(2,1)}) %reduce-scatter.3.cloned.1.call-update) | async-done | bytes 917520 | tf_op jit(solution)/shard_map/reduce_scatter | solution.py:15
  371.2 0.0 copy-done
  371.2 2.4 fusion.1
  373.6 0.0 reduce-scatter.5.cloned.1.call-update
  374.3 27.6 %reduce-scatter.5.cloned.1.call-done = bf16[224,512]{1,0:T(8,128)(2,1)} async-done(((bf16[224,2048]{1,0:T(8,128)(2,1)}), bf16[224,512]{1,0:T(8,128)(2,1)}) %reduce-scatter.5.cloned.1.call-update) | async-done | bytes 229392 | tf_op jit(solution)/shard_map/reduce_scatter | solution.py:25
  401.9 1.4 fusion.2
  403.3 10.9 %all_gather.7 = bf16[224,2048]{1,0:T(8,128)(2,1)S(1)} all-gather(bf16[224,512]{1,0:T(8,128)(2,1)S(1)} %get-tuple-element.2), channel_id=1, replica_groups=mesh['island'=4,'fsdp'=32] {'island'}, dimensions={1}, use_global_device_ids=true | all-gather | bytes 1146880 | tf_op jit(solution)/shard_map/all_gather | solution.py:40
  414.3 1.4 convert_element_type.41
  415.7 10.9 %all_gather.6 = bf16[224,2048]{1,0:T(8,128)(2,1)S(1)} all-gather(bf16[224,512]{1,0:T(8,128)(2,1)S(1)} %get-tuple-element.3), channel_id=1, replica_groups=mesh['island'=4,'fsdp'=32] {'island'}, dimensions={1}, use_global_device_ids=true | all-gather | bytes 1146880 | tf_op jit(solution)/shard_map/all_gather | solution.py:37
  426.6 0.9 copy.11
Async XLA Ops:
  7.2 364.1 %reduce-scatter.3.cloned.1.call-start = ((), (), s32[]{:S(2)}) async-start(), calls=%async_computation.2 | async-start | bytes 30277632 | tf_op jit(solution)/shard_map/reduce_scatter | solution.py:15
  46.7 0.7 copy-start.1
  46.7 324.6 %copy-start = (f32[1,224,2048]{2,1,0:T(8,128)S(1)}, f32[1,224,2048]{2,1,0:T(8,128)}, u32[]{:S(2)}) copy-start(f32[1,224,2048]{2,1,0:T(8,128)} %param.9) | copy-start | bytes 5505028
  46.7 355.2 %reduce-scatter.5.cloned.1.call-start = ((), (), s32[]{:S(2)}) async-start(), calls=%async_computation.3 | async-start | bytes 1146880 | tf_op jit(solution)/shard_map/reduce_scatter | solution.py:25
Sparse Core Ops, SparseCore 0:
  46.8 324.3 reduce-scatter.2
  374.5 27.3 reduce-scatter.4
where the time goes:
time: 435 us; the launch traced here: 434 us
  waiting for transfers between devices  350 us (80%)
  matrix products  39.4 us (9%)
  blocking collectives  21.9 us (5%)
  between operations  15.3 us (4%)
  other arithmetic  5.9 us (1%)
    reduce_scatter x1, waiting for transfers between devices, body(): lax.psum_scatter(product.astype(jnp.bfloat16), 'fsdp', scatter_dimension=...  323 us
    dot_general x1, matrix products, body(): lax.dot_general(hidden_acts, output_grads, (((0,), (0,)), ((), ())), pref...  39.4 us
    reduce_scatter x1, waiting for transfers between devices, body(): lax.psum_scatter(weighted.astype(jnp.bfloat16), 'island', scatter_dimensi...  27.6 us
    all_gather x1, blocking collectives, body(): lax.all_gather(new_moment.astype(jnp.bfloat16), 'island', axis=1, tiled=T...  10.9 us
    all_gather x1, blocking collectives, body(): lax.all_gather(new_master.astype(jnp.bfloat16), 'island', axis=1, tiled=T...  10.9 us
  transfers between devices with their start and end apart: 2, of which 2 were waited for; matrix products, arithmetic and copies ran while one was open for 0% of the time, Pallas kernels for 0%

commit v1 on v0

v1 whole, which is shorter than its diff:
```python
import functools

import jax
import jax.numpy as jnp
import numpy as np
from jax import lax
from jax.experimental import pallas as pl
from jax.experimental.pallas import tpu as pltpu
from jax.sharding import PartitionSpec as P

inner_rate = 0.5
outer_decay = 0.9
outer_rate = 0.7

AXES = ("island", "fsdp")
RING = 4
BLOCKS = 64
COLS = 256
PANELS = 4
PARTS = 3

ORDERS = tuple(
    tuple(((p + k) % 3, bit) for bit in range(2) for k in range(3)) for p in range(PARTS)
)


def gray(v):
    return v ^ (v >> 1)


def place(axis_values):
    y, z, x, core = axis_values
    return ((x // 2) * 2 + core) * 32 + y * 8 + (x % 2) * 4 + z


def permutation(move):
    pairs = []
    for y in range(RING):
        for z in range(RING):
            for x in range(RING):
                for core in range(2):
                    pairs.append((place((y, z, x, core)), place(move(y, z, x, core))))
    return pairs


def neighbour(axis, bit):
    def move(y, z, x, core):
        at = [y, z, x]
        at[axis] = gray(gray_flip(at[axis], bit ^ core))
        return (*at, core)

    return permutation(move)


def gray_flip(v, bit):
    return gray(v) ^ (1 << bit)


def swap_core(y, z, x, core):
    return y, z, x, 1 - core


def opposite(y, z, x, core):
    return y, z, x ^ 2, core


def block_table(y, z, x, core):
    rows = []
    for part in range(PARTS):
        at = [jnp.full((BLOCKS,), gray(v), jnp.int32) for v in (y, z, x)]
        for step, (axis, bit) in enumerate(ORDERS[part]):
            taken = jnp.asarray((np.arange(BLOCKS) >> (5 - step)) & 1, jnp.int32)
            at[axis] = at[axis] ^ (taken << (bit ^ core))
        by, bz = at[0] ^ (at[0] >> 1), at[1] ^ (at[1] >> 1)
        half = at[2] >> 1
        low = (at[2] & 1) ^ half
        rows.append(((by * 2 + low) * RING + bz) * 2 + half)
    return jnp.stack(rows)


def transpose_kernel(acts, out):
    step = pl.program_id(0)
    turned = acts[...].T
    out[pl.ds(step * 8, 8)] = turned.reshape(8, turned.shape[0] // 8, turned.shape[1])


def transposed(acts):
    tokens, hidden = acts.shape
    width = hidden // 8
    return pl.pallas_call(
        transpose_kernel,
        grid=(8,),
        in_specs=[pl.BlockSpec((tokens, width), lambda j: (0, j))],
        out_specs=pl.BlockSpec(memory_space=pltpu.VMEM),
        out_shape=pltpu.VMEM((BLOCKS, hidden // BLOCKS, tokens), acts.dtype),
        compiler_params=pltpu.CompilerParams(vmem_limit_bytes=16 << 20),
        cost_estimate=pl.CostEstimate(
            flops=0, bytes_accessed=2 * acts.size, transcendentals=0
        ),
        name="transpose_acts",
    )(acts)


def panel_kernel(first, row_lo, row_n, table, acts, main, shared, scale, *rest):
    out = rest[-1]
    step = pl.program_id(0)
    rows = acts.shape[1]
    picks = [table[first + step * 8 + b] for b in range(8)]
    left = jnp.concatenate([acts[at] for at in picks], axis=0)
    left_shared = jnp.concatenate([acts[at, row_lo : row_lo + row_n] for at in picks], axis=0)
    factor = scale[0]
    top = jnp.dot(left, main[...], preferred_element_type=jnp.float32) * factor
    low = jnp.dot(left_shared, shared[...], preferred_element_type=jnp.float32) * factor
    top = top.reshape(8, rows, COLS)
    low = low.reshape(8, row_n, COLS)
    if len(rest) == 2:
        top = top + rest[0][:, :rows].astype(jnp.float32)
        low = low + rest[0][:, rows:].astype(jnp.float32)
    out[:, :rows] = top.astype(out.dtype)
    out[:, rows:] = low.astype(out.dtype)


SHARED_ROWS = ((0, 48), (48, 32), (80, 32))


def panel(acts, grads, table, scale, part, half, received=None):
    row_lo, row_n = SHARED_ROWS[part]
    tokens = acts.shape[2]
    height = acts.shape[1] + row_n
    block = pl.BlockSpec((8, height, COLS), lambda i, t: (i, 0, 0))
    more = () if received is None else (received,)
    return pl.pallas_call(
        functools.partial(panel_kernel, half * 32, row_lo, row_n),
        grid_spec=pltpu.PrefetchScalarGridSpec(
            num_scalar_prefetch=1,
            grid=(4,),
            in_specs=[
                pl.BlockSpec(memory_space=pltpu.VMEM),
                pl.BlockSpec((tokens, COLS), lambda i, t: (0, t[BLOCKS] * PANELS + part)),
                pl.BlockSpec((tokens, COLS), lambda i, t: (0, t[BLOCKS] * PANELS + 3)),
                pl.BlockSpec(memory_space=pltpu.SMEM),
            ]
            + [block] * len(more),
            out_specs=block,
        ),
        out_shape=jax.ShapeDtypeStruct((32, height, COLS), jnp.bfloat16),
        compiler_params=pltpu.CompilerParams(vmem_limit_bytes=16 << 20),
        cost_estimate=pl.CostEstimate(
            flops=2 * 32 * height * COLS * tokens,
            bytes_accessed=2 * 32 * height * COLS * (2 if more else 1) + 4 * tokens * COLS,
            transcendentals=0,
        ),
        name=f"panel_{part}_{half}_{len(more)}",
    )(table, acts, grads, grads, scale, *more)


def send(value, pairs):
    return lax.ppermute(value, AXES, pairs)


def total(terms):
    out = terms[0].astype(jnp.float32)
    for term in terms[1:]:
        out = out + term.astype(jnp.float32)
    return out


def after(value, *others):
    return lax.optimization_barrier((value, *others))[0]


def body(hidden_acts, output_grads, island_drift, master_weights, momentum, mixture, denominator):
    island = lax.axis_index("island")
    fsdp = lax.axis_index("fsdp")
    core = island % 2
    x_hi = island // 2
    y = fsdp // 8
    x = x_hi * 2 + (fsdp // 4) % 2
    z = fsdp % 4
    weight = lax.dynamic_slice(mixture, (island,), (1,)).astype(jnp.float32)
    tables = [
        [jnp.concatenate([t, jnp.full((1,), 0, jnp.int32) + who]) for t in block_table(y, z, x, who)]
        for who in (core, 1 - core)
    ]
    swap = permutation(swap_core)

    width = PANELS * COLS
    drift = island_drift[0] * weight[0]
    keep = lax.dynamic_slice_in_dim(drift, core * width, width, 1)
    give = lax.dynamic_slice_in_dim(drift, (1 - core) * width, width, 1)
    keep = keep + send(give.astype(jnp.bfloat16), swap).astype(jnp.float32)
    rows = keep.shape[0] // 2
    give = lax.dynamic_slice_in_dim(keep, (1 - x_hi) * rows, rows, 0)
    keep = lax.dynamic_slice_in_dim(keep, x_hi * rows, rows, 0)
    drift_sum = keep + send(give.astype(jnp.bfloat16), permutation(opposite)).astype(jnp.float32)

    acts = transposed(hidden_acts)
    chain = [acts]

    def product(part, half, theirs, received=None):
        table = after(tables[theirs][part], chain[-1])
        out = panel(acts, output_grads, table, weight, part, half, received)
        chain.append(out)
        return out

    arrived = [send(product(p, 1, 1), swap) for p in range(PARTS)]
    first = [product(p, 1, 0, arrived[p]) for p in range(PARTS)]
    got = [[send(first[p], neighbour(*ORDERS[p][0]))] for p in range(PARTS)]
    arrived = [send(product(p, 0, 1), swap) for p in range(PARTS)]
    local = [product(p, 0, 0, arrived[p]) for p in range(PARTS)]

    for step in range(1, 6):
        size = 32 >> step
        for p in range(PARTS):
            terms = [local[p]] + got[p]
            out = total([t[size : 2 * size] for t in terms]).astype(jnp.bfloat16)
            got[p].append(send(out, neighbour(*ORDERS[p][step])))
    sums = [total([t[0] for t in [local[p]] + got[p]]) for p in range(PARTS)]
    shared = jnp.concatenate([s[rows:] for s in sums], axis=0)
    gradient = jnp.concatenate([s[:rows] for s in sums] + [shared], axis=1)

    divisor = denominator[0].astype(jnp.float32)
    mine = ((drift_sum + inner_rate * gradient) / divisor).astype(jnp.bfloat16)
    other = send(mine, permutation(opposite))
    half = jnp.where(
        x_hi == 0,
        jnp.concatenate([mine, other], axis=0),
        jnp.concatenate([other, mine], axis=0),
    )
    beside = send(half, swap)
    combined = jnp.where(
        core == 0,
        jnp.concatenate([half, beside], axis=1),
        jnp.concatenate([beside, half], axis=1),
    ).astype(jnp.float32)
    new_moment = outer_decay * momentum + combined
    new_master = master_weights - outer_rate * (combined + outer_decay * new_moment)
    return new_master.astype(jnp.bfloat16), new_moment


def solution(mesh):
    in_specs = (
        P(("island", "fsdp"), None),
        P(("island", "fsdp"), None),
        P("island", "fsdp", None),
        P("fsdp", None),
        P("fsdp", None),
        P(),
        P(),
    )
    out_specs = (P("fsdp", None), P("fsdp", None))
    return jax.shard_map(body, mesh=mesh, in_specs=in_specs, out_specs=out_specs, check_vma=False)
```

time: 435 us -> 192 us (0.44)
  waiting for transfers between devices: 350 us -> 47.4 us
  Pallas kernels: 0 us -> 53.4 us
  starting transfers between devices: 0.08 us -> 40.4 us
  matrix products: 39.4 us -> 0 us
  other arithmetic: 5.9 us -> 29.6 us
  blocking collectives: 21.9 us -> 0 us
  local copies, waits for them, and re-layouts: 1.5 us -> 18.1 us
  between operations: 15.3 us -> 2.46 us
    reduce_scatter x2 -> x0, waiting for transfers between devices: 350 us -> none  [the longest x1 323 us: body(): lax.psum_scatter(product.astype(jnp.bfloat16), 'fsdp', scatter_dimension=...]
    pallas_call x0 -> x13, Pallas kernels: none -> 53.4 us  [the longest x12 48.4 us: panel(): pl.pallas_call(functools.partial(panel_kernel, half * 32, row_lo, row_n),...]
    ppermute x0 -> x28, waiting for transfers between devices: none -> 47.4 us  [send(): return lax.ppermute(value, AXES, pairs)]
    ppermute x0 -> x28, starting transfers between devices: none -> 40.4 us  [send(): return lax.ppermute(value, AXES, pairs)]
    dot_general x1 -> x0, matrix products: 39.4 us -> none  [body(): lax.dot_general(hidden_acts, output_grads, (((0,), (0,)), ((), ())), pref...]
    all_gather x2 -> x0, blocking collectives: 21.9 us -> none  [the longest x1 10.9 us: body(): lax.all_gather(new_moment.astype(jnp.bfloat16), 'island', axis=1, tiled=T...]
    convert_element_type x3 -> x17, other arithmetic: 5.27 us -> 24.3 us  [the longest x15 19.9 us: body(): out = total([t[size:2 * size] for t in terms]).astype(jnp.bfloat16)]
    unnamed x5 -> x40, local copies, waits for them, and re-layouts: 1.5 us -> 17.4 us
  transfers between devices with their start and end apart: 2 -> 28, of which waited for: 2 -> 13; matrix products, arithmetic and copies ran while one was open for 0% -> 13% of each run, Pallas kernels for 0% -> 19%
where the time goes in v1:
time: 192 us; the launch traced here: 191 us
  Pallas kernels  53.4 us (28%)
  waiting for transfers between devices  47.4 us (25%)
  starting transfers between devices  40.4 us (21%)
  other arithmetic  29.6 us (15%)
  local copies, waits for them, and re-layouts  18.1 us (9%)
  between operations  2.46 us (1%)
    pallas_call x12, Pallas kernels, panel(): pl.pallas_call(functools.partial(panel_kernel, half * 32, row_lo, row_n),...  48.4 us
    ppermute x28, waiting for transfers between devices, send(): return lax.ppermute(value, AXES, pairs)  47.4 us
    ppermute x28, starting transfers between devices, send(): return lax.ppermute(value, AXES, pairs)  40.4 us
    convert_element_type x15, other arithmetic, body(): out = total([t[size:2 * size] for t in terms]).astype(jnp.bfloat16)  19.9 us
    unnamed x40, local copies, waits for them, and re-layouts  17.4 us
    pallas_call x1, Pallas kernels, transposed(): pl.pallas_call(transpose_kernel, grid=(8,), in_specs=[pl.BlockSpec((token...  5.08 us
    convert_element_type x1, other arithmetic, body(): return (new_master.astype(jnp.bfloat16), new_moment)  4.26 us
  transfers between devices with their start and end apart: 28, of which 13 were waited for; matrix products, arithmetic and copies ran while one was open for 13% of the time, Pallas kernels for 19%

profile of v1, /device:TPU:1, one launch (start us, length us, event | category | flops | bytes accessed | tf_op | source)
XLA Modules:
  0.0 191.4 jit_solution(14120059916053029823)
XLA Ops:
  0.7 4.6 %copy-done.4 = bf16[896,7168]{1,0:T(8,128)(2,1)S(1)} copy-done((bf16[896,7168]{1,0:T(8,128)(2,1)S(1)}, bf16[896,7168]{1,0:T(8,128)(2,1)}, u32[]{:S(2)}) %copy-start.4) | copy-done | bytes 12845080
  5.4 5.1 %transpose_acts.1.acts = bf16[64,112,896]{2,1,0:T(8,128)(2,1)S(1)} custom-call(bf16[896,7168]{1,0:T(8,128)(2,1)S(1)} %copy-done.4), custom_call_target="tpu_custom_call" | custom-call | bytes 12845056 | tf_op jit(solution)/shard_map/transpose_acts/pallas_call | solution.py:90
  10.5 4.6 %copy-done = bf16[64,112,896]{2,1,0:T(8,128)(2,1)} copy-done((bf16[64,112,896]{2,1,0:T(8,128)(2,1)}, bf16[64,112,896]{2,1,0:T(8,128)(2,1)S(1)}, u32[]{:S(2)}) %copy-start) | copy-done | bytes 12845080
  15.3 0.6 dynamic_slice.17
  16.4 4.6 %copy-done.1 = bf16[64,112,896]{2,1,0:T(8,128)(2,1)S(1)} copy-done((bf16[64,112,896]{2,1,0:T(8,128)(2,1)S(1)}, bf16[64,112,896]{2,1,0:T(8,128)(2,1)}, u32[]{:S(2)}) %copy-start.1) | copy-done | bytes 12845080
  21.1 2.0 %copy-done.2 = bf16[896,2048]{1,0:T(8,128)(2,1)S(1)} copy-done((bf16[896,2048]{1,0:T(8,128)(2,1)S(1)}, bf16[896,2048]{1,0:T(8,128)(2,1)}, u32[]{:S(2)}) %copy-start.2) | copy-done | bytes 3670040
  23.1 4.2 %panel_0_1_0.1 = bf16[32,160,256]{2,1,0:T(8,128)(2,1)S(1)} custom-call(s32[65]{0:T(128)S(1)} %pad_add_fusion.3.table, bf16[64,112,896]{2,1,0:T(8,128)(2,1)S(1)} %copy-done.1, bf16[896,2048]{1,0:T(8,128)(2,1)S(1)} %copy-done.2, bf16[896,2048]{1,0:T(8,128)(2,1)S(1)} %copy-done.2, f32[1]{0:T(128)} %convert_element_type.360.scale), custom_call_target="tpu_custom_call" | custom-call | flops 2348810240 | bytes 3538944 | tf_op jit(solution)/shard_map/panel_0_1_0/pallas_call | solution.py:132
  27.3 1.5 collective-permute-start.2
  28.9 3.9 %panel_1_1_0.1 = bf16[32,144,256]{2,1,0:T(8,128)(2,1)S(1)} custom-call(s32[65]{0:T(128)S(1)} %get-tuple-element.21.table, bf16[64,112,896]{2,1,0:T(8,128)(2,1)S(1)} %copy-done.1, bf16[896,2048]{1,0:T(8,128)(2,1)S(1)} %copy-done.2, bf16[896,2048]{1,0:T(8,128)(2,1)S(1)} %copy-done.2, f32[1]{0:T(128)} %convert_element_type.360.scale), custom_call_target="tpu_custom_call" | custom-call | flops 2113929216 | bytes 3276800 | tf_op jit(solution)/shard_map/panel_1_1_0/pallas_call | solution.py:132
  32.9 3.9 %panel_2_1_0.1 = bf16[32,144,256]{2,1,0:T(8,128)(2,1)S(1)} custom-call(s32[65]{0:T(128)S(1)} %get-tuple-element.22.table, bf16[64,112,896]{2,1,0:T(8,128)(2,1)S(1)} %copy-done.1, bf16[896,2048]{1,0:T(8,128)(2,1)S(1)} %copy-done.3, bf16[896,2048]{1,0:T(8,128)(2,1)S(1)} %copy-done.3, f32[1]{0:T(128)} %convert_element_type.360.scale), custom_call_target="tpu_custom_call" | custom-call | flops 2113929216 | bytes 3276800 | tf_op jit(solution)/shard_map/panel_2_1_0/pallas_call | solution.py:132
  37.7 4.2 %panel_0_1_1.1 = bf16[32,160,256]{2,1,0:T(8,128)(2,1)S(1)} custom-call(s32[65]{0:T(128)S(1)} %pad_add_fusion.table, bf16[64,112,896]{2,1,0:T(8,128)(2,1)S(1)} %copy-done.1, bf16[896,2048]{1,0:T(8,128)(2,1)S(1)} %copy-done.3, bf16[896,2048]{1,0:T(8,128)(2,1)S(1)} %copy-done.3, f32[1]{0:T(128)} %convert_element_type.360.scale, ...), custom_call_target="tpu_custom_call" | custom-call | flops 2348810240 | bytes 6160384 | tf_op jit(solution)/shard_map/panel_0_1_1/pallas_call | solution.py:132
  41.9 4.0 %panel_1_1_1.1 = bf16[32,144,256]{2,1,0:T(8,128)(2,1)S(1)} custom-call(s32[65]{0:T(128)S(1)} %pad_add_fusion.5.table, bf16[64,112,896]{2,1,0:T(8,128)(2,1)S(1)} %copy-done.1, bf16[896,2048]{1,0:T(8,128)(2,1)S(1)} %copy-done.3, bf16[896,2048]{1,0:T(8,128)(2,1)S(1)} %copy-done.3, f32[1]{0:T(128)} %convert_element_type.360.scale, ...), custom_call_target="tpu_custom_call" | custom-call | flops 2113929216 | bytes 5636096 | tf_op jit(solution)/shard_map/panel_1_1_1/pallas_call | solution.py:132
  45.9 4.0 %panel_2_1_1.1 = bf16[32,144,256]{2,1,0:T(8,128)(2,1)S(1)} custom-call(s32[65]{0:T(128)S(1)} %pad_add_fusion.4.table, bf16[64,112,896]{2,1,0:T(8,128)(2,1)S(1)} %copy-done.1, bf16[896,2048]{1,0:T(8,128)(2,1)S(1)} %copy-done.3, bf16[896,2048]{1,0:T(8,128)(2,1)S(1)} %copy-done.3, f32[1]{0:T(128)} %convert_element_type.360.scale, ...), custom_call_target="tpu_custom_call" | custom-call | flops 2113929216 | bytes 5636096 | tf_op jit(solution)/shard_map/panel_2_1_1/pallas_call | solution.py:132
  49.9 4.2 %panel_0_0_0.1 = bf16[32,160,256]{2,1,0:T(8,128)(2,1)S(1)} custom-call(s32[65]{0:T(128)S(1)} %pad_add_fusion.3.table, bf16[64,112,896]{2,1,0:T(8,128)(2,1)S(1)} %copy-done.1, bf16[896,2048]{1,0:T(8,128)(2,1)S(1)} %copy-done.3, bf16[896,2048]{1,0:T(8,128)(2,1)S(1)} %copy-done.3, f32[1]{0:T(128)} %convert_element_type.360.scale), custom_call_target="tpu_custom_call" | custom-call | flops 2348810240 | bytes 3538944 | tf_op jit(solution)/shard_map/panel_0_0_0/pallas_call | solution.py:132
  54.2 3.9 %panel_1_0_0.1 = bf16[32,144,256]{2,1,0:T(8,128)(2,1)S(1)} custom-call(s32[65]{0:T(128)S(1)} %get-tuple-element.21.table, bf16[64,112,896]{2,1,0:T(8,128)(2,1)S(1)} %copy-done.1, bf16[896,2048]{1,0:T(8,128)(2,1)S(1)} %copy-done.3, bf16[896,2048]{1,0:T(8,128)(2,1)S(1)} %copy-done.3, f32[1]{0:T(128)} %convert_element_type.360.scale), custom_call_target="tpu_custom_call" | custom-call | flops 2113929216 | bytes 3276800 | tf_op jit(solution)/shard_map/panel_1_0_0/pallas_call | solution.py:132
  58.1 0.6 collective-permute-start.12
  58.7 3.9 %panel_2_0_0.1 = bf16[32,144,256]{2,1,0:T(8,128)(2,1)S(1)} custom-call(s32[65]{0:T(128)S(1)} %get-tuple-element.22.table, bf16[64,112,896]{2,1,0:T(8,128)(2,1)S(1)} %copy-done.1, bf16[896,2048]{1,0:T(8,128)(2,1)S(1)} %copy-done.3, bf16[896,2048]{1,0:T(8,128)(2,1)S(1)} %copy-done.3, f32[1]{0:T(128)} %convert_element_type.360.scale), custom_call_target="tpu_custom_call" | custom-call | flops 2113929216 | bytes 3276800 | tf_op jit(solution)/shard_map/panel_2_0_0/pallas_call | solution.py:132
  62.7 2.7 %collective-permute-start.20 = (bf16[32,144,256]{2,1,0:T(8,128)(2,1)S(1)}, bf16[32,144,256]{2,1,0:T(8,128)(2,1)S(1)}, u32[]{:S(2)}, u32[]{:S(2)}) collective-permute-start(bf16[32,144,256]{2,1,0:T(8,128)(2,1)S(1)} %panel_2_1_1.1), channel_id=1, source_target_pairs={{0,4},{32,100},{4,0},{36,96},{64,68},{96,36},{68,64},{100,32},{1,5... | collective-permute-start | bytes 7077896 | tf_op jit(solution)/shard_map/ppermute | solution.py:158
  65.4 3.7 %collective-permute-start.13 = (bf16[32,144,256]{2,1,0:T(8,128)(2,1)S(1)}, bf16[32,144,256]{2,1,0:T(8,128)(2,1)S(1)}, u32[]{:S(2)}, u32[]{:S(2)}) collective-permute-start(bf16[32,144,256]{2,1,0:T(8,128)(2,1)S(1)} %panel_1_1_1.1), channel_id=1, source_target_pairs={{0,1},{32,35},{4,5},{36,39},{64,65},{96,99},{68,69},{100,103},{1,0... | collective-permute-start | bytes 7077896 | tf_op jit(solution)/shard_map/ppermute | solution.py:158
  69.1 2.7 %collective-permute-start.6 = (bf16[32,160,256]{2,1,0:T(8,128)(2,1)S(1)}, bf16[32,160,256]{2,1,0:T(8,128)(2,1)S(1)}, u32[]{:S(2)}, u32[]{:S(2)}) collective-permute-start(bf16[32,160,256]{2,1,0:T(8,128)(2,1)S(1)} %panel_0_1_1.1), channel_id=1, source_target_pairs={{0,8},{32,56},{4,12},{36,60},{64,72},{96,120},{68,76},{100,124},{1... | collective-permute-start | bytes 7864328 | tf_op jit(solution)/shard_map/ppermute | solution.py:158
  71.8 4.2 %panel_0_0_1.1 = bf16[32,160,256]{2,1,0:T(8,128)(2,1)S(1)} custom-call(s32[65]{0:T(128)S(1)} %pad_add_fusion.table, bf16[64,112,896]{2,1,0:T(8,128)(2,1)S(1)} %copy-done.1, bf16[896,2048]{1,0:T(8,128)(2,1)S(1)} %copy-done.3, bf16[896,2048]{1,0:T(8,128)(2,1)S(1)} %copy-done.3, f32[1]{0:T(128)} %convert_element_type.360.scale, ...), custom_call_target="tpu_custom_call" | custom-call | flops 2348810240 | bytes 6160384 | tf_op jit(solution)/shard_map/panel_0_0_1/pallas_call | solution.py:132
  76.1 4.0 %panel_1_0_1.1 = bf16[32,144,256]{2,1,0:T(8,128)(2,1)S(1)} custom-call(s32[65]{0:T(128)S(1)} %pad_add_fusion.5.table, bf16[64,112,896]{2,1,0:T(8,128)(2,1)S(1)} %copy-done.1, bf16[896,2048]{1,0:T(8,128)(2,1)S(1)} %copy-done.3, bf16[896,2048]{1,0:T(8,128)(2,1)S(1)} %copy-done.3, f32[1]{0:T(128)} %convert_element_type.360.scale, ...), custom_call_target="tpu_custom_call" | custom-call | flops 2113929216 | bytes 5636096 | tf_op jit(solution)/shard_map/panel_1_0_1/pallas_call | solution.py:132
  80.1 4.0 %panel_2_0_1.1 = bf16[32,144,256]{2,1,0:T(8,128)(2,1)S(1)} custom-call(s32[65]{0:T(128)S(1)} %pad_add_fusion.4.table, bf16[64,112,896]{2,1,0:T(8,128)(2,1)S(1)} %copy-done.1, bf16[896,2048]{1,0:T(8,128)(2,1)S(1)} %copy-done.3, bf16[896,2048]{1,0:T(8,128)(2,1)S(1)} %copy-done.3, f32[1]{0:T(128)} %convert_element_type.360.scale, ...), custom_call_target="tpu_custom_call" | custom-call | flops 2113929216 | bytes 5636096 | tf_op jit(solution)/shard_map/panel_2_0_1/pallas_call | solution.py:132
  84.0 7.6 %collective-permute-done.20 = bf16[32,144,256]{2,1,0:T(8,128)(2,1)S(1)} collective-permute-done((bf16[32,144,256]{2,1,0:T(8,128)(2,1)S(1)}, bf16[32,144,256]{2,1,0:T(8,128)(2,1)S(1)}, u32[]{:S(2)}, u32[]{:S(2)}) %collective-permute-start.20) | collective-permute-done | bytes 2359328 | tf_op jit(solution)/shard_map/ppermute | solution.py:158
  91.7 1.7 add_convert_fusion.1
  93.4 2.8 %collective-permute-start.21 = (bf16[16,144,256]{2,1,0:T(8,128)(2,1)}, bf16[16,144,256]{2,1,0:T(8,128)(2,1)}, u32[]{:S(2)}, u32[]{:S(2)}) collective-permute-start(bf16[16,144,256]{2,1,0:T(8,128)(2,1)} %add_convert_fusion.1), channel_id=1, source_target_pairs={{0,8},{32,56},{4,12},{36,60},{64,72},{96,120},{68,76},{100,124},{1... | collective-permute-start | bytes 3538952 | tf_op jit(solution)/shard_map/ppermute | solution.py:158
  96.2 1.7 add_convert_fusion.2
  97.9 2.5 %collective-permute-start.14 = (bf16[16,144,256]{2,1,0:T(8,128)(2,1)}, bf16[16,144,256]{2,1,0:T(8,128)(2,1)}, u32[]{:S(2)}, u32[]{:S(2)}) collective-permute-start(bf16[16,144,256]{2,1,0:T(8,128)(2,1)} %add_convert_fusion.2), channel_id=1, source_target_pairs={{0,4},{32,100},{4,0},{36,96},{64,68},{96,36},{68,64},{100,32},{1,5... | collective-permute-start | bytes 3538952 | tf_op jit(solution)/shard_map/ppermute | solution.py:158
  100.9 1.8 add_convert_fusion
  102.8 3.3 %collective-permute-start.7 = (bf16[16,160,256]{2,1,0:T(8,128)(2,1)}, bf16[16,160,256]{2,1,0:T(8,128)(2,1)}, u32[]{:S(2)}, u32[]{:S(2)}) collective-permute-start(bf16[16,160,256]{2,1,0:T(8,128)(2,1)} %add_convert_fusion), channel_id=1, source_target_pairs={{0,1},{32,35},{4,5},{36,39},{64,65},{96,99},{68,69},{100,103},{1,0... | collective-permute-start | bytes 3932168 | tf_op jit(solution)/shard_map/ppermute | solution.py:158
  106.1 1.7 broadcast_multiply_fusion
  107.7 1.2 copy-done.8
  109.8 3.8 %collective-permute-done.21 = bf16[16,144,256]{2,1,0:T(8,128)(2,1)} collective-permute-done((bf16[16,144,256]{2,1,0:T(8,128)(2,1)}, bf16[16,144,256]{2,1,0:T(8,128)(2,1)}, u32[]{:S(2)}, u32[]{:S(2)}) %collective-permute-start.21) | collective-permute-done | bytes 1179680 | tf_op jit(solution)/shard_map/ppermute | solution.py:158
  113.6 1.6 add_convert_fusion.4
  115.6 1.5 add_convert_fusion.5
  117.1 2.8 %collective-permute-start.15 = (bf16[8,144,256]{2,1,0:T(8,128)(2,1)S(1)}, bf16[8,144,256]{2,1,0:T(8,128)(2,1)S(1)}, u32[]{:S(2)}, u32[]{:S(2)}) collective-permute-start(bf16[8,144,256]{2,1,0:T(8,128)(2,1)S(1)} %add_convert_fusion.5), channel_id=1, source_target_pairs={{0,8},{32,56},{4,12},{36,60},{64,72},{96,120},{68,76},{100,124},{1... | collective-permute-start | bytes 1769480 | tf_op jit(solution)/shard_map/ppermute | solution.py:158
  119.8 1.5 collective-permute-done.7
  121.4 1.5 add_convert_fusion.3
  122.9 1.0 collective-permute-start.8
  124.4 3.2 %collective-permute-done.22 = bf16[8,144,256]{2,1,0:T(8,128)(2,1)S(1)} collective-permute-done((bf16[8,144,256]{2,1,0:T(8,128)(2,1)S(1)}, bf16[8,144,256]{2,1,0:T(8,128)(2,1)S(1)}, u32[]{:S(2)}, u32[]{:S(2)}) %collective-permute-start.22) | collective-permute-done | bytes 589856 | tf_op jit(solution)/shard_map/ppermute | solution.py:158
  127.6 1.3 add_convert_fusion.7
  129.0 1.2 add_convert_fusion.8
  130.3 11.7 %collective-permute-done.8 = bf16[8,160,256]{2,1,0:T(8,128)(2,1)S(1)} collective-permute-done((bf16[8,160,256]{2,1,0:T(8,128)(2,1)S(1)}, bf16[8,160,256]{2,1,0:T(8,128)(2,1)S(1)}, u32[]{:S(2)}, u32[]{:S(2)}) %collective-permute-start.8) | collective-permute-done | bytes 655392 | tf_op jit(solution)/shard_map/ppermute | solution.py:158
  142.0 1.2 add_convert_fusion.6
  143.3 1.2 add_convert_fusion.10
  144.5 1.5 collective-permute-start.24
  146.0 1.1 add_convert_fusion.11
  147.2 3.9 %collective-permute-done.24 = bf16[2,144,256]{2,1,0:T(8,128)(2,1)S(1)} collective-permute-done((bf16[2,144,256]{2,1,0:T(8,128)(2,1)S(1)}, bf16[2,144,256]{2,1,0:T(8,128)(2,1)S(1)}, u32[]{:S(2)}, u32[]{:S(2)}) %collective-permute-start.24) | collective-permute-done | bytes 147488 | tf_op jit(solution)/shard_map/ppermute | solution.py:158
  151.1 1.0 add_convert_fusion.13
  152.2 1.0 add_convert_fusion.14
  153.3 2.1 %collective-permute-done.25 = bf16[1,144,256]{2,1,0:T(8,128)(2,1)S(1)} collective-permute-done((bf16[1,144,256]{2,1,0:T(8,128)(2,1)S(1)}, bf16[1,144,256]{2,1,0:T(8,128)(2,1)S(1)}, u32[]{:S(2)}, u32[]{:S(2)}) %collective-permute-start.25) | collective-permute-done | bytes 73760 | tf_op jit(solution)/shard_map/ppermute | solution.py:158
  155.4 1.0 add_add_fusion.1
  156.5 1.0 add_add_fusion.2
  157.6 1.1 add_convert_fusion.9
  158.7 1.8 collective-permute-start.10
  160.5 2.7 %collective-permute-done.10 = bf16[2,160,256]{2,1,0:T(8,128)(2,1)S(1)} collective-permute-done((bf16[2,160,256]{2,1,0:T(8,128)(2,1)S(1)}, bf16[2,160,256]{2,1,0:T(8,128)(2,1)S(1)}, u32[]{:S(2)}, u32[]{:S(2)}) %collective-permute-start.10) | collective-permute-done | bytes 163872 | tf_op jit(solution)/shard_map/ppermute | solution.py:158
  163.2 1.0 add_convert_fusion.12
  164.3 3.3 %collective-permute-done.11 = bf16[1,160,256]{2,1,0:T(8,128)(2,1)S(1)} collective-permute-done((bf16[1,160,256]{2,1,0:T(8,128)(2,1)S(1)}, bf16[1,160,256]{2,1,0:T(8,128)(2,1)S(1)}, u32[]{:S(2)}, u32[]{:S(2)}) %collective-permute-start.11) | collective-permute-done | bytes 81952 | tf_op jit(solution)/shard_map/ppermute | solution.py:158
  167.6 1.0 add_add_fusion
  168.7 1.0 collective-permute-start.26
  169.7 5.6 %collective-permute-done.26 = bf16[112,1024]{1,0:T(8,128)(2,1)S(1)} collective-permute-done((bf16[112,1024]{1,0:T(8,128)(2,1)S(1)}, bf16[112,1024]{1,0:T(8,128)(2,1)S(1)}, u32[]{:S(2)}, u32[]{:S(2)}) %collective-permute-start.26) | collective-permute-done | bytes 229408 | tf_op jit(solution)/shard_map/ppermute | solution.py:158
  175.4 10.3 %collective-permute-start.27 = (bf16[224,1024]{1,0:T(8,128)(2,1)S(1)}, bf16[224,1024]{1,0:T(8,128)(2,1)S(1)}, u32[]{:S(2)}, u32[]{:S(2)}) collective-permute-start(bf16[224,1024]{1,0:T(8,128)(2,1)S(1)} %maximum_select_fusion.1), channel_id=1, source_target_pairs={{0,32},{32,0},{4,36},{36,4},{64,96},{96,64},{68,100},{100,68},{1,3... | collective-permute-start | bytes 1376264 | tf_op jit(solution)/shard_map/ppermute | solution.py:158
  185.7 1.4 collective-permute-done.27
  187.1 4.3 %fusion.2 = (bf16[224,2048]{1,0:T(8,128)(2,1)}, f32[224,2048]{1,0:T(8,128)}) fusion(f32[224,2048]{1,0:T(8,128)} %param.46, bf16[224,1024]{1,0:T(8,128)(2,1)S(1)} %maximum_select_fusion.1, bf16[224,1024]{1,0:T(8,128)(2,1)S(1)} %collective-permute-done.27, pred[]{:T(512)S(6)} %eq.10, f32[224,2048]{1,0:T(8,128)} %param.47), kind=kLoop, calls=%fused_computation.7 | loop fusion | flops 7798784 | bytes 7340033 | tf_op jit(solution)/shard_map/convert_element_type | solution.py:238
  (83 shorter events, 3.8 us)
Async XLA Ops:
  0.7 4.7 %copy-start.4 = (bf16[896,7168]{1,0:T(8,128)(2,1)S(1)}, bf16[896,7168]{1,0:T(8,128)(2,1)}, u32[]{:S(2)}) copy-start(bf16[896,7168]{1,0:T(8,128)(2,1)} %acts.1) | copy-start | bytes 38535172
  5.4 9.8 %copy-start.13 = (s32[64]{0:T(128)S(1)}, s32[64]{0:T(128)}, u32[]{:S(2)}) copy-start(s32[64]{0:T(128)} %constant.102.clone) | copy-start | bytes 772
  5.4 9.8 %copy-start.14 = (s32[64]{0:T(128)S(1)}, s32[64]{0:T(128)}, u32[]{:S(2)}) copy-start(s32[64]{0:T(128)} %constant.99.clone) | copy-start | bytes 772
  5.4 9.8 %copy-start.15 = (s32[64]{0:T(128)S(1)}, s32[64]{0:T(128)}, u32[]{:S(2)}) copy-start(s32[64]{0:T(128)} %constant.101.clone) | copy-start | bytes 772
  5.4 9.8 %copy-start.16 = (s32[64]{0:T(128)S(1)}, s32[64]{0:T(128)}, u32[]{:S(2)}) copy-start(s32[64]{0:T(128)} %constant.98.clone) | copy-start | bytes 772
  5.4 9.8 %copy-start.17 = (s32[64]{0:T(128)S(1)}, s32[64]{0:T(128)}, u32[]{:S(2)}) copy-start(s32[64]{0:T(128)} %constant.103.clone) | copy-start | bytes 772
  5.4 9.8 %copy-start.18 = (s32[64]{0:T(128)S(1)}, s32[64]{0:T(128)}, u32[]{:S(2)}) copy-start(s32[64]{0:T(128)} %constant.100.clone) | copy-start | bytes 772
  5.4 9.9 %copy-start.19 = (s32[4]{0:T(128)S(1)}, s32[4]{0:T(128)}, u32[]{:S(2)}) copy-start(s32[4]{0:T(128)} %param.48) | copy-start | bytes 52
  10.5 4.6 %copy-start = (bf16[64,112,896]{2,1,0:T(8,128)(2,1)}, bf16[64,112,896]{2,1,0:T(8,128)(2,1)S(1)}, u32[]{:S(2)}) copy-start(bf16[64,112,896]{2,1,0:T(8,128)(2,1)S(1)} %transpose_acts.1.acts) | copy-start | bytes 38535172
  16.4 4.7 %copy-start.1 = (bf16[64,112,896]{2,1,0:T(8,128)(2,1)S(1)}, bf16[64,112,896]{2,1,0:T(8,128)(2,1)}, u32[]{:S(2)}) copy-start(bf16[64,112,896]{2,1,0:T(8,128)(2,1)} %copy-done) | copy-start | bytes 38535172
  21.1 2.0 %copy-start.2 = (bf16[896,2048]{1,0:T(8,128)(2,1)S(1)}, bf16[896,2048]{1,0:T(8,128)(2,1)}, u32[]{:S(2)}) copy-start(bf16[896,2048]{1,0:T(8,128)(2,1)} %shared.23) | copy-start | bytes 11010052
  27.3 10.3 %collective-permute-start.2 = (bf16[32,160,256]{2,1,0:T(8,128)(2,1)S(1)}, bf16[32,160,256]{2,1,0:T(8,128)(2,1)S(1)}, u32[]{:S(2)}, u32[]{:S(2)}) collective-permute-start(bf16[32,160,256]{2,1,0:T(8,128)(2,1)S(1)} %panel_0_1_0.1), channel_id=1, source_target_pairs={{0,32},{32,0},{4,36},{36,4},{64,96},{96,64},{68,100},{100,68},{1,3... | collective-permute-start | bytes 7864328 | tf_op jit(solution)/shard_map/ppermute | solution.py:158
  28.9 4.0 %copy-start.3 = (bf16[896,2048]{1,0:T(8,128)(2,1)S(1)}, bf16[896,2048]{1,0:T(8,128)(2,1)}, u32[]{:S(2)}) copy-start(bf16[896,2048]{1,0:T(8,128)(2,1)} %shared.23) | copy-start | bytes 11010052
  32.8 9.1 %collective-permute-start.3 = (bf16[32,144,256]{2,1,0:T(8,128)(2,1)S(1)}, bf16[32,144,256]{2,1,0:T(8,128)(2,1)S(1)}, u32[]{:S(2)}, u32[]{:S(2)}) collective-permute-start(bf16[32,144,256]{2,1,0:T(8,128)(2,1)S(1)} %panel_1_1_0.1), channel_id=1, source_target_pairs={{0,32},{32,0},{4,36},{36,4},{64,96},{96,64},{68,100},{100,68},{1,3... | collective-permute-start | bytes 7077896 | tf_op jit(solution)/shard_map/ppermute | solution.py:158
  36.9 9.0 %collective-permute-start.4 = (bf16[32,144,256]{2,1,0:T(8,128)(2,1)S(1)}, bf16[32,144,256]{2,1,0:T(8,128)(2,1)S(1)}, u32[]{:S(2)}, u32[]{:S(2)}) collective-permute-start(bf16[32,144,256]{2,1,0:T(8,128)(2,1)S(1)} %panel_2_1_0.1), channel_id=1, source_target_pairs={{0,32},{32,0},{4,36},{36,4},{64,96},{96,64},{68,100},{100,68},{1,3... | collective-permute-start | bytes 7077896 | tf_op jit(solution)/shard_map/ppermute | solution.py:158
  54.1 15.0 %collective-permute-start.5 = (bf16[32,160,256]{2,1,0:T(8,128)(2,1)S(1)}, bf16[32,160,256]{2,1,0:T(8,128)(2,1)S(1)}, u32[]{:S(2)}, u32[]{:S(2)}) collective-permute-start(bf16[32,160,256]{2,1,0:T(8,128)(2,1)S(1)} %panel_0_0_0.1), channel_id=1, source_target_pairs={{0,32},{32,0},{4,36},{36,4},{64,96},{96,64},{68,100},{100,68},{1,3... | collective-permute-start | bytes 7864328 | tf_op jit(solution)/shard_map/ppermute | solution.py:158
  58.1 18.0 %collective-permute-start.12 = (bf16[32,144,256]{2,1,0:T(8,128)(2,1)S(1)}, bf16[32,144,256]{2,1,0:T(8,128)(2,1)S(1)}, u32[]{:S(2)}, u32[]{:S(2)}) collective-permute-start(bf16[32,144,256]{2,1,0:T(8,128)(2,1)S(1)} %panel_1_0_0.1), channel_id=1, source_target_pairs={{0,32},{32,0},{4,36},{36,4},{64,96},{96,64},{68,100},{100,68},{1,3... | collective-permute-start | bytes 7077896 | tf_op jit(solution)/shard_map/ppermute | solution.py:158
  62.6 17.5 %collective-permute-start.19 = (bf16[32,144,256]{2,1,0:T(8,128)(2,1)S(1)}, bf16[32,144,256]{2,1,0:T(8,128)(2,1)S(1)}, u32[]{:S(2)}, u32[]{:S(2)}) collective-permute-start(bf16[32,144,256]{2,1,0:T(8,128)(2,1)S(1)} %panel_2_0_0.1), channel_id=1, source_target_pairs={{0,32},{32,0},{4,36},{36,4},{64,96},{96,64},{68,100},{100,68},{1,3... | collective-permute-start | bytes 7077896 | tf_op jit(solution)/shard_map/ppermute | solution.py:158
  62.7 29.0 %collective-permute-start.20 = (bf16[32,144,256]{2,1,0:T(8,128)(2,1)S(1)}, bf16[32,144,256]{2,1,0:T(8,128)(2,1)S(1)}, u32[]{:S(2)}, u32[]{:S(2)}) collective-permute-start(bf16[32,144,256]{2,1,0:T(8,128)(2,1)S(1)} %panel_2_1_1.1), channel_id=1, source_target_pairs={{0,4},{32,100},{4,0},{36,96},{64,68},{96,36},{68,64},{100,32},{1,5... | collective-permute-start | bytes 7077896 | tf_op jit(solution)/shard_map/ppermute | solution.py:158
  65.4 30.8 %collective-permute-start.13 = (bf16[32,144,256]{2,1,0:T(8,128)(2,1)S(1)}, bf16[32,144,256]{2,1,0:T(8,128)(2,1)S(1)}, u32[]{:S(2)}, u32[]{:S(2)}) collective-permute-start(bf16[32,144,256]{2,1,0:T(8,128)(2,1)S(1)} %panel_1_1_1.1), channel_id=1, source_target_pairs={{0,1},{32,35},{4,5},{36,39},{64,65},{96,99},{68,69},{100,103},{1,0... | collective-permute-start | bytes 7077896 | tf_op jit(solution)/shard_map/ppermute | solution.py:158
  69.1 31.8 %collective-permute-start.6 = (bf16[32,160,256]{2,1,0:T(8,128)(2,1)S(1)}, bf16[32,160,256]{2,1,0:T(8,128)(2,1)S(1)}, u32[]{:S(2)}, u32[]{:S(2)}) collective-permute-start(bf16[32,160,256]{2,1,0:T(8,128)(2,1)S(1)} %panel_0_1_1.1), channel_id=1, source_target_pairs={{0,8},{32,56},{4,12},{36,60},{64,72},{96,120},{68,76},{100,124},{1... | collective-permute-start | bytes 7864328 | tf_op jit(solution)/shard_map/ppermute | solution.py:158
  80.0 16.1 %copy-start.5 = (bf16[32,144,256]{2,1,0:T(8,128)(2,1)}, bf16[32,144,256]{2,1,0:T(8,128)(2,1)S(1)}, u32[]{:S(2)}) copy-start(bf16[32,144,256]{2,1,0:T(8,128)(2,1)S(1)} %panel_1_0_1.1) | copy-start | bytes 7077892
  84.0 13.9 %copy-start.7 = (bf16[32,144,256]{2,1,0:T(8,128)(2,1)}, bf16[32,144,256]{2,1,0:T(8,128)(2,1)S(1)}, u32[]{:S(2)}) copy-start(bf16[32,144,256]{2,1,0:T(8,128)(2,1)S(1)} %panel_2_0_1.1) | copy-start | bytes 7077892
  91.7 6.2 %copy-start.12 = (bf16[32,144,256]{2,1,0:T(8,128)(2,1)}, bf16[32,144,256]{2,1,0:T(8,128)(2,1)S(1)}, u32[]{:S(2)}) copy-start(bf16[32,144,256]{2,1,0:T(8,128)(2,1)S(1)} %collective-permute-done.20) | copy-start | bytes 7077892
  93.4 20.2 %collective-permute-start.21 = (bf16[16,144,256]{2,1,0:T(8,128)(2,1)}, bf16[16,144,256]{2,1,0:T(8,128)(2,1)}, u32[]{:S(2)}, u32[]{:S(2)}) collective-permute-start(bf16[16,144,256]{2,1,0:T(8,128)(2,1)} %add_convert_fusion.1), channel_id=1, source_target_pairs={{0,8},{32,56},{4,12},{36,60},{64,72},{96,120},{68,76},{100,124},{1... | collective-permute-start | bytes 3538952 | tf_op jit(solution)/shard_map/ppermute | solution.py:158
  96.2 6.5 %copy-start.11 = (bf16[32,144,256]{2,1,0:T(8,128)(2,1)}, bf16[32,144,256]{2,1,0:T(8,128)(2,1)S(1)}, u32[]{:S(2)}) copy-start(bf16[32,144,256]{2,1,0:T(8,128)(2,1)S(1)} %collective-permute-done.13) | copy-start | bytes 7077892
  97.9 17.7 %collective-permute-start.14 = (bf16[16,144,256]{2,1,0:T(8,128)(2,1)}, bf16[16,144,256]{2,1,0:T(8,128)(2,1)}, u32[]{:S(2)}, u32[]{:S(2)}) collective-permute-start(bf16[16,144,256]{2,1,0:T(8,128)(2,1)} %add_convert_fusion.2), channel_id=1, source_target_pairs={{0,4},{32,100},{4,0},{36,96},{64,68},{96,36},{68,64},{100,32},{1,5... | collective-permute-start | bytes 3538952 | tf_op jit(solution)/shard_map/ppermute | solution.py:158
  100.9 1.9 %copy-start.10 = (bf16[32,160,256]{2,1,0:T(8,128)(2,1)}, bf16[32,160,256]{2,1,0:T(8,128)(2,1)S(1)}, u32[]{:S(2)}) copy-start(bf16[32,160,256]{2,1,0:T(8,128)(2,1)S(1)} %collective-permute-done.6) | copy-start | bytes 7864324
  102.8 18.6 %collective-permute-start.7 = (bf16[16,160,256]{2,1,0:T(8,128)(2,1)}, bf16[16,160,256]{2,1,0:T(8,128)(2,1)}, u32[]{:S(2)}, u32[]{:S(2)}) collective-permute-start(bf16[16,160,256]{2,1,0:T(8,128)(2,1)} %add_convert_fusion), channel_id=1, source_target_pairs={{0,1},{32,35},{4,5},{36,39},{64,65},{96,99},{68,69},{100,103},{1,0... | collective-permute-start | bytes 3932168 | tf_op jit(solution)/shard_map/ppermute | solution.py:158
  107.7 1.2 copy-start.8
  109.0 14.9 %collective-permute-start = (bf16[224,1024]{1,0:T(8,128)(2,1)S(1)}, bf16[224,1024]{1,0:T(8,128)(2,1)S(1)}, u32[]{:S(2)}, u32[]{:S(2)}) collective-permute-start(bf16[224,1024]{1,0:T(8,128)(2,1)S(1)} %fusion.3), channel_id=1, source_target_pairs={{0,32},{32,0},{4,36},{36,4},{64,96},{96,64},{68,100},{100,68},{1,3... | collective-permute-start | bytes 1376264 | tf_op jit(solution)/shard_map/ppermute | solution.py:158
  109.8 5.8 %copy-start.6 = (bf16[32,144,256]{2,1,0:T(8,128)(2,1)S(1)}, bf16[32,144,256]{2,1,0:T(8,128)(2,1)}, u32[]{:S(2)}) copy-start(bf16[32,144,256]{2,1,0:T(8,128)(2,1)} %copy-done.5) | copy-start | bytes 7077892
  115.2 12.3 %collective-permute-start.22 = (bf16[8,144,256]{2,1,0:T(8,128)(2,1)S(1)}, bf16[8,144,256]{2,1,0:T(8,128)(2,1)S(1)}, u32[]{:S(2)}, u32[]{:S(2)}) collective-permute-start(bf16[8,144,256]{2,1,0:T(8,128)(2,1)S(1)} %add_convert_fusion.4), channel_id=1, source_target_pairs={{0,1},{32,35},{4,5},{36,39},{64,65},{96,99},{68,69},{100,103},{1,0... | collective-permute-start | bytes 1769480 | tf_op jit(solution)/shard_map/ppermute | solution.py:158
  117.1 6.9 %copy-start.9 = (f32[1,224,2048]{2,1,0:T(8,128)S(1)}, f32[1,224,2048]{2,1,0:T(8,128)}, u32[]{:S(2)}) copy-start(f32[1,224,2048]{2,1,0:T(8,128)} %copy-done.8) | copy-start | bytes 5505028
  117.1 11.9 %collective-permute-start.15 = (bf16[8,144,256]{2,1,0:T(8,128)(2,1)S(1)}, bf16[8,144,256]{2,1,0:T(8,128)(2,1)S(1)}, u32[]{:S(2)}, u32[]{:S(2)}) collective-permute-start(bf16[8,144,256]{2,1,0:T(8,128)(2,1)S(1)} %add_convert_fusion.5), channel_id=1, source_target_pairs={{0,8},{32,56},{4,12},{36,60},{64,72},{96,120},{68,76},{100,124},{1... | collective-permute-start | bytes 1769480 | tf_op jit(solution)/shard_map/ppermute | solution.py:158
  122.9 19.1 %collective-permute-start.8 = (bf16[8,160,256]{2,1,0:T(8,128)(2,1)S(1)}, bf16[8,160,256]{2,1,0:T(8,128)(2,1)S(1)}, u32[]{:S(2)}, u32[]{:S(2)}) collective-permute-start(bf16[8,160,256]{2,1,0:T(8,128)(2,1)S(1)} %add_convert_fusion.3), channel_id=1, source_target_pairs={{0,4},{32,100},{4,0},{36,96},{64,68},{96,36},{68,64},{100,32},{1,5... | collective-permute-start | bytes 1966088 | tf_op jit(solution)/shard_map/ppermute | solution.py:158
  124.1 44.5 %collective-permute-start.1 = (bf16[112,1024]{1,0:T(8,128)(2,1)S(1)}, bf16[112,1024]{1,0:T(8,128)(2,1)S(1)}, u32[]{:S(2)}, u32[]{:S(2)}) collective-permute-start(bf16[112,1024]{1,0:T(8,128)(2,1)S(1)} %dynamic-slice_convert_fusion.1), channel_id=1, source_target_pairs={{0,64},{32,96},{4,68},{36,100},{64,0},{96,32},{68,4},{100,36},{1,6... | collective-permute-start | bytes 688136 | tf_op jit(solution)/shard_map/ppermute | solution.py:158
  128.9 14.4 %collective-permute-start.23 = (bf16[4,144,256]{2,1,0:T(8,128)(2,1)S(1)}, bf16[4,144,256]{2,1,0:T(8,128)(2,1)S(1)}, u32[]{:S(2)}, u32[]{:S(2)}) collective-permute-start(bf16[4,144,256]{2,1,0:T(8,128)(2,1)S(1)} %add_convert_fusion.7), channel_id=1, source_target_pairs={{0,68},{32,36},{4,64},{36,32},{64,4},{96,100},{68,0},{100,96},{1,6... | collective-permute-start | bytes 884744 | tf_op jit(solution)/shard_map/ppermute | solution.py:158
  130.2 15.8 %collective-permute-start.16 = (bf16[4,144,256]{2,1,0:T(8,128)(2,1)S(1)}, bf16[4,144,256]{2,1,0:T(8,128)(2,1)S(1)}, u32[]{:S(2)}, u32[]{:S(2)}) collective-permute-start(bf16[4,144,256]{2,1,0:T(8,128)(2,1)S(1)} %add_convert_fusion.8), channel_id=1, source_target_pairs={{0,3},{32,33},{4,7},{36,37},{64,67},{96,97},{68,71},{100,101},{1,2... | collective-permute-start | bytes 884744 | tf_op jit(solution)/shard_map/ppermute | solution.py:158
  143.2 14.3 %collective-permute-start.9 = (bf16[4,160,256]{2,1,0:T(8,128)(2,1)S(1)}, bf16[4,160,256]{2,1,0:T(8,128)(2,1)S(1)}, u32[]{:S(2)}, u32[]{:S(2)}) collective-permute-start(bf16[4,160,256]{2,1,0:T(8,128)(2,1)S(1)} %add_convert_fusion.6), channel_id=1, source_target_pairs={{0,24},{32,40},{4,28},{36,44},{64,88},{96,104},{68,92},{100,108},{... | collective-permute-start | bytes 983048 | tf_op jit(solution)/shard_map/ppermute | solution.py:158
  144.5 6.6 %collective-permute-start.24 = (bf16[2,144,256]{2,1,0:T(8,128)(2,1)S(1)}, bf16[2,144,256]{2,1,0:T(8,128)(2,1)S(1)}, u32[]{:S(2)}, u32[]{:S(2)}) collective-permute-start(bf16[2,144,256]{2,1,0:T(8,128)(2,1)S(1)} %add_convert_fusion.10), channel_id=1, source_target_pairs={{0,24},{32,40},{4,28},{36,44},{64,88},{96,104},{68,92},{100,108},{... | collective-permute-start | bytes 442376 | tf_op jit(solution)/shard_map/ppermute | solution.py:158
  147.1 5.1 %collective-permute-start.17 = (bf16[2,144,256]{2,1,0:T(8,128)(2,1)S(1)}, bf16[2,144,256]{2,1,0:T(8,128)(2,1)S(1)}, u32[]{:S(2)}, u32[]{:S(2)}) collective-permute-start(bf16[2,144,256]{2,1,0:T(8,128)(2,1)S(1)} %add_convert_fusion.11), channel_id=1, source_target_pairs={{0,68},{32,36},{4,64},{36,32},{64,4},{96,100},{68,0},{100,96},{1,6... | collective-permute-start | bytes 442376 | tf_op jit(solution)/shard_map/ppermute | solution.py:158
  152.1 3.3 %collective-permute-start.25 = (bf16[1,144,256]{2,1,0:T(8,128)(2,1)S(1)}, bf16[1,144,256]{2,1,0:T(8,128)(2,1)S(1)}, u32[]{:S(2)}, u32[]{:S(2)}) collective-permute-start(bf16[1,144,256]{2,1,0:T(8,128)(2,1)S(1)} %add_convert_fusion.13), channel_id=1, source_target_pairs={{0,3},{32,33},{4,7},{36,37},{64,67},{96,97},{68,71},{100,101},{1,2... | collective-permute-start | bytes 221192 | tf_op jit(solution)/shard_map/ppermute | solution.py:158
  153.2 3.3 %collective-permute-start.18 = (bf16[1,144,256]{2,1,0:T(8,128)(2,1)S(1)}, bf16[1,144,256]{2,1,0:T(8,128)(2,1)S(1)}, u32[]{:S(2)}, u32[]{:S(2)}) collective-permute-start(bf16[1,144,256]{2,1,0:T(8,128)(2,1)S(1)} %add_convert_fusion.14), channel_id=1, source_target_pairs={{0,24},{32,40},{4,28},{36,44},{64,88},{96,104},{68,92},{100,108},{... | collective-permute-start | bytes 221192 | tf_op jit(solution)/shard_map/ppermute | solution.py:158
  158.7 4.5 %collective-permute-start.10 = (bf16[2,160,256]{2,1,0:T(8,128)(2,1)S(1)}, bf16[2,160,256]{2,1,0:T(8,128)(2,1)S(1)}, u32[]{:S(2)}, u32[]{:S(2)}) collective-permute-start(bf16[2,160,256]{2,1,0:T(8,128)(2,1)S(1)} %add_convert_fusion.9), channel_id=1, source_target_pairs={{0,3},{32,33},{4,7},{36,37},{64,67},{96,97},{68,71},{100,101},{1,2... | collective-permute-start | bytes 491528 | tf_op jit(solution)/shard_map/ppermute | solution.py:158
  164.2 3.4 %collective-permute-start.11 = (bf16[1,160,256]{2,1,0:T(8,128)(2,1)S(1)}, bf16[1,160,256]{2,1,0:T(8,128)(2,1)S(1)}, u32[]{:S(2)}, u32[]{:S(2)}) collective-permute-start(bf16[1,160,256]{2,1,0:T(8,128)(2,1)S(1)} %add_convert_fusion.12), channel_id=1, source_target_pairs={{0,68},{32,36},{4,64},{36,32},{64,4},{96,100},{68,0},{100,96},{1,6... | collective-permute-start | bytes 245768 | tf_op jit(solution)/shard_map/ppermute | solution.py:158
  168.7 6.6 %collective-permute-start.26 = (bf16[112,1024]{1,0:T(8,128)(2,1)S(1)}, bf16[112,1024]{1,0:T(8,128)(2,1)S(1)}, u32[]{:S(2)}, u32[]{:S(2)}) collective-permute-start(bf16[112,1024]{1,0:T(8,128)(2,1)S(1)} %fusion.6), channel_id=1, source_target_pairs={{0,64},{32,96},{4,68},{36,100},{64,0},{96,32},{68,4},{100,36},{1,6... | collective-permute-start | bytes 688136 | tf_op jit(solution)/shard_map/ppermute | solution.py:158
  175.4 11.7 %collective-permute-start.27 = (bf16[224,1024]{1,0:T(8,128)(2,1)S(1)}, bf16[224,1024]{1,0:T(8,128)(2,1)S(1)}, u32[]{:S(2)}, u32[]{:S(2)}) collective-permute-start(bf16[224,1024]{1,0:T(8,128)(2,1)S(1)} %maximum_select_fusion.1), channel_id=1, source_target_pairs={{0,32},{32,0},{4,36},{36,4},{64,96},{96,64},{68,100},{100,68},{1,3... | collective-permute-start | bytes 1376264 | tf_op jit(solution)/shard_map/ppermute | solution.py:158
